TPU v7x, 32 devices: a whole 2x2x4 slice. The times are simulated.
32 devices in a mesh: dp: 4 (over z), uly: 4 (over y, core), blk: 2 (over x).
Axes of the slice: x: 2, y: 2, z: 4, core: 2. Of those that a mesh axis runs over, the one named last changes fastest.
Arguments:
- query_rows: bfloat16 [8, 256, 3072], P(('dp', 'blk'), 'uly'), parts along dimension 0, may hold values from -400 to 400
- key_rows: bfloat16 [8, 256, 3072], P(('dp', 'blk'), 'uly'), parts along dimension 0, may hold values from -400 to 400
- value_rows: bfloat16 [8, 256, 3072], P(('dp', 'blk'), 'uly'), parts along dimension 0, may hold values from -6 to 6
- norm_query: float32 [3072], replicated, may hold values from 1 to 2.2
- norm_key: float32 [3072], replicated, may hold values from 1 to 2.2
- out_weight: bfloat16 [3072, 5120], P('blk', 'uly'), may hold values from -0.109375 to 0.109375
- out_bias: float32 [5120], P('uly'), may hold values from -3 to 3
- gate: float32 [5120], P('uly'), may hold values from 0.3 to 1.5
- residual: bfloat16 [8, 256, 5120], P(('dp', 'blk'), None, 'uly'), parts along dimension 0, may hold values from -3 to 3
Outputs:
- mixed: bfloat16 [8, 256, 5120], P(('dp', 'blk'), None, 'uly'), parts along dimension 0
There are 4 independent parts, one for each index of `dp`. A program takes and returns all parts, laid end to end along the dimension named above; an argument that names none is the same for every part. Nothing has to cross between parts.
All inputs are finite; a program needn't handle non-finite values.
Results may differ from a plain program's by a relative error of at most 0.011.
Values may be sent and summed in bfloat16 or wider, within the bound.
A program may use at most 64 MiB of HBM per device.

v0:
```python
import jax
import jax.numpy as jnp
from jax import lax
from jax.sharding import PartitionSpec as P

HEAD = 128


EPS = 1e-06


def normalize(rows_in, gain):
    wide = rows_in.astype(jnp.float32)
    factor = lax.rsqrt(jnp.mean(wide * wide, axis=-1, keepdims=True) + EPS)
    return (wide * factor * gain).astype(jnp.bfloat16)


def split_heads(array):
    return array.reshape(array.shape[0], array.shape[1] // HEAD, HEAD)


def initial_state(queries):
    count = queries.shape[1]
    length = queries.shape[0]
    return (
        jnp.full((count, length), -1e30, jnp.float32),
        jnp.zeros((count, length), jnp.float32),
        jnp.zeros((count, length, HEAD), jnp.float32),
    )


def absorb(state, keys, values, queries):
    peak, total, accum = state
    scores = jnp.einsum(
        "qhd,khd->hqk", queries, keys, preferred_element_type=jnp.float32
    ) * HEAD ** (-0.5)
    new_peak = jnp.maximum(peak, jnp.max(scores, axis=2))
    factor = jnp.exp(peak - new_peak)
    weights = jnp.exp(scores - new_peak[:, :, None])
    total = total * factor + jnp.sum(weights, axis=2)
    accum = accum * factor[:, :, None] + jnp.einsum(
        "hqk,khd->hqd", weights.astype(jnp.bfloat16), values, preferred_element_type=jnp.float32
    )
    return (new_peak, total, accum)


def attend(state, keys, values, queries):
    length = keys.shape[0]
    stride = 512
    count = keys.shape[1] // HEAD
    key_blocks = keys.reshape(length // stride, stride, count, HEAD)
    value_blocks = values.reshape(length // stride, stride, count, HEAD)

    def visit(carry, pair):
        return (absorb(carry, pair[0], pair[1], queries), None)

    state, unused = lax.scan(visit, state, (key_blocks, value_blocks))
    return state


def shards(
    query_rows, key_rows, value_rows, norm_query, norm_key, out_weight, out_bias, gate, residual
):
    local_query = normalize(query_rows[0], norm_query)
    local_key = normalize(key_rows[0], norm_key)
    local_value = value_rows[0]
    head_query = lax.all_to_all(local_query, "uly", split_axis=1, concat_axis=0, tiled=True)
    head_key, head_value = (
        lax.all_to_all(local_key, "uly", split_axis=1, concat_axis=0, tiled=True),
        lax.all_to_all(local_value, "uly", split_axis=1, concat_axis=0, tiled=True),
    )
    queries = split_heads(head_query)
    state = attend(
        initial_state(queries),
        lax.all_gather(head_key, "blk", axis=0, tiled=True),
        lax.all_gather(head_value, "blk", axis=0, tiled=True),
        queries,
    )
    peak, total, accum = state
    length = queries.shape[0]
    attended = (accum / total[:, :, None]).astype(jnp.bfloat16)
    attended = attended.transpose(1, 0, 2).reshape(length, queries.shape[1] * HEAD)
    gathered = lax.all_gather(attended, "uly", axis=1, tiled=True)
    projected = jnp.dot(
        gathered,
        lax.all_gather(out_weight, "blk", axis=0, tiled=True),
        preferred_element_type=jnp.float32,
    )
    mixed = residual[0].astype(jnp.float32) + gate * (projected + out_bias)
    return mixed.astype(jnp.bfloat16)[None]


def solution(mesh):
    placed = (
        P(("dp", "blk"), "uly", None),
        P(("dp", "blk"), "uly", None),
        P(("dp", "blk"), "uly", None),
        P(),
        P(),
        P("blk", "uly"),
        P("uly"),
        P("uly"),
        P(("dp", "blk"), None, "uly"),
    )
    return jax.shard_map(
        shards, mesh=mesh, in_specs=placed, out_specs=P(("dp", "blk"), None, "uly"), check_vma=False
    )
```

profile of v0, /device:TPU:0, one launch (start us, length us, event | category | flops | bytes accessed | tf_op | source)
XLA Modules:
  0.0 202.0 jit_solution(3511442398119196197)
XLA Ops:
  6.5 0.0 copy-start
  6.5 0.0 copy-start.3
  6.5 1.4 reshape.90
  8.0 1.2 multiply_reduce_fusion.1
  9.1 0.7 mul.94
  9.9 0.0 copy-start.2
  9.9 0.2 multiply_convert_fusion
  10.1 0.8 copy.24
  10.9 4.2 %all-to-all-start.1 = ((bf16[64,4,768]{2,0,1:T(8,128)(2,1)}), bf16[64,4,768]{2,0,1:T(8,128)(2,1)S(1)}, u32[]{:S(2)}, u32[]{:S(2)}) async-start(bf16[64,4,768]{2,0,1:T(8,128)(2,1)} %copy.24), calls=%async_computation.1 | async-start | bytes 786432 | tf_op jit(solution)/shard_map/all_to_all | solution.py:69
  15.1 0.0 copy-done
  15.2 0.2 multiply_reduce_fusion.2
  15.3 0.4 reshape.89
  15.7 0.0 copy-done.3
  15.8 1.0 fusion.23
  16.8 5.8 %all-to-all-done.1 = bf16[64,4,768]{2,0,1:T(8,128)(2,1)S(1)} async-done(((bf16[64,4,768]{2,0,1:T(8,128)(2,1)}), bf16[64,4,768]{2,0,1:T(8,128)(2,1)S(1)}, u32[]{:S(2)}, u32[]{:S(2)}) %all-to-all-start.1) | async-done | bytes 393248 | tf_op jit(solution)/shard_map/all_to_all | solution.py:69
  22.6 3.5 %all-to-all-start = ((bf16[64,4,768]{2,0,1:T(8,128)(2,1)}), bf16[64,4,768]{2,0,1:T(8,128)(2,1)S(1)}, u32[]{:S(2)}, u32[]{:S(2)}) async-start(bf16[64,4,768]{2,0,1:T(8,128)(2,1)} %fusion.23), calls=%async_computation | async-start | bytes 786432 | tf_op jit(solution)/shard_map/all_to_all | solution.py:67
  26.1 0.0 copy-done.2
  26.1 0.3 all_to_all.41
  26.4 0.8 copy.28
  27.2 12.5 %all_gather.12 = bf16[512,768]{1,0:T(8,128)(2,1)S(1)} all-gather(bf16[256,768]{1,0:T(8,128)(2,1)S(1)} %bitcast.35), channel_id=1, replica_groups=mesh['dp'=4,'uly'=4,'blk'=2] {'blk'}, dimensions={0}, use_global_device_ids=true | all-gather | bytes 1179648 | tf_op jit(solution)/shard_map/all_gather | solution.py:75
  39.7 1.2 copy.25
  40.9 0.0 all-to-all-done
  40.9 3.5 %all-to-all-start.2 = ((bf16[64,4,768]{2,0,1:T(8,128)(2,1)}), bf16[64,4,768]{2,0,1:T(8,128)(2,1)S(1)}, u32[]{:S(2)}, u32[]{:S(2)}) async-start(bf16[64,4,768]{2,0,1:T(8,128)(2,1)} %copy.28), calls=%async_computation.2 | async-start | bytes 786432 | tf_op jit(solution)/shard_map/all_to_all | solution.py:70
  44.3 0.0 all-gather.3.cloned.1.call-start
  44.4 1.2 reshape.86
  45.6 1.9 multiply_reduce_fusion
  47.6 0.9 fusion.3
  48.5 0.6 bitcast_add_fusion
  49.1 2.6 %all-to-all-done.2 = bf16[64,4,768]{2,0,1:T(8,128)(2,1)S(1)} async-done(((bf16[64,4,768]{2,0,1:T(8,128)(2,1)}), bf16[64,4,768]{2,0,1:T(8,128)(2,1)S(1)}, u32[]{:S(2)}, u32[]{:S(2)}) %all-to-all-start.2) | async-done | bytes 393248 | tf_op jit(solution)/shard_map/all_to_all | solution.py:70
  51.7 11.4 %all_gather.13 = bf16[512,768]{1,0:T(8,128)(2,1)} all-gather(bf16[256,768]{1,0:T(8,128)(2,1)S(1)} %bitcast.36), channel_id=1, replica_groups=mesh['dp'=4,'uly'=4,'blk'=2] {'blk'}, dimensions={0}, use_global_device_ids=true | all-gather | bytes 1179648 | tf_op jit(solution)/shard_map/all_gather | solution.py:76
  63.2 2.3 %copy.29 = bf16[512,768]{0,1:T(8,128)(2,1)} copy(bf16[512,768]{1,0:T(8,128)(2,1)} %all_gather.13) | data formatting | bytes 1572864 | tf_op jit(solution)/shard_map/all_gather | solution.py:76
  65.5 2.8 %fusion.19 = bf16[256,6,128]{0,2,1:T(8,128)(2,1)} fusion(bf16[512,6,128]{0,2,1:T(8,128)(2,1)} %bitcast.37, f32[6,256,512]{2,1,0:T(8,128)S(1)} %get-tuple-element.20, f32[6,256]{1,0:T(8,128)S(1)} %get-tuple-element.18, f32[256,6]{0,1:T(8,128)} %bitcast_add_fusion, f32[256,6]{0,1:T(8,128)S(1)} %get-tuple-element.17), kind=kOutput, calls=%fused_computation.15 | convolution fusion | flops 204275712 | bytes 4343808 | tf_op jit(solution)/shard_map/while/body/eval_jaxpr/hqk,khd->hqd/dot_general | solution.py:41
  68.2 0.0 copy-start.1
  68.2 0.0 copy-start.4
  68.2 0.0 copy-start.5
  68.2 0.0 all-gather.3.cloned.1.call-update
  68.3 0.0 all-gather.5.cloned.1.call-start
  68.3 0.7 all-gather.5.cloned.1.call-update
  69.0 19.7 %all-gather.3.cloned.1.call-done = bf16[256,3072]{0,1:T(8,128)(2,1)} async-done(((bf16[256,768]{0,1:T(8,128)(2,1)}), bf16[256,3072]{0,1:T(8,128)(2,1)}) %all-gather.3.cloned.1.call-update) | async-done | bytes 1572880 | tf_op jit(solution)/shard_map/all_gather | solution.py:83
  88.7 99.7 %all-gather.5.cloned.1.call-done = bf16[3072,1280]{1,0:T(8,128)(2,1)} async-done(((bf16[1536,1280]{1,0:T(8,128)(2,1)}), bf16[3072,1280]{1,0:T(8,128)(2,1)}) %all-gather.5.cloned.1.call-update) | async-done | bytes 7864336 | tf_op jit(solution)/shard_map/all_gather | solution.py:86
  188.4 0.0 copy-done.1
  188.4 0.0 copy-done.4
  188.4 0.0 copy-done.5
  188.4 6.8 %fusion.5 = bf16[1,256,1280]{2,1,0:T(8,128)(2,1)} fusion(bf16[256,3072]{0,1:T(8,128)(2,1)} %all-gather.3.cloned.1.call-done, bf16[3072,1280]{1,0:T(8,128)(2,1)} %all-gather.5.cloned.1.call-done, bf16[1,256,1280]{2,1,0:T(8,128)(2,1)S(1)} %copy-done.1, f32[1280]{0:T(1024)S(1)} %copy-done.4, f32[1280]{0:T(1024)S(1)} %copy-done.5), kind=kOutput, calls=%fused_computation.8 | convolution fusion | flops 2014904320 | bytes 10758144 | tf_op jit(solution)/shard_map/dot_general | solution.py:84
  (4 shorter events, 0.0 us)
Async XLA Ops:
  6.5 8.6 %copy-start = (bf16[1,64,3072]{2,1,0:T(8,128)(2,1)S(1)}, bf16[1,64,3072]{2,1,0:T(8,128)(2,1)}, u32[]{:S(2)}) copy-start(bf16[1,64,3072]{2,1,0:T(8,128)(2,1)} %param.9) | copy-start | bytes 1179652
  6.5 9.2 %copy-start.3 = (f32[3072]{0:T(1024)S(1)}, f32[3072]{0:T(1024)}, u32[]{:S(2)}) copy-start(f32[3072]{0:T(1024)} %param.12) | copy-start | bytes 36868
  9.9 16.2 %copy-start.2 = (bf16[1,64,3072]{2,1,0:T(8,128)(2,1)S(1)}, bf16[1,64,3072]{2,1,0:T(8,128)(2,1)}, u32[]{:S(2)}) copy-start(bf16[1,64,3072]{2,1,0:T(8,128)(2,1)} %param.11) | copy-start | bytes 1179652
  10.9 11.7 %all-to-all-start.1 = ((bf16[64,4,768]{2,0,1:T(8,128)(2,1)}), bf16[64,4,768]{2,0,1:T(8,128)(2,1)S(1)}, u32[]{:S(2)}, u32[]{:S(2)}) async-start(bf16[64,4,768]{2,0,1:T(8,128)(2,1)} %copy.24), calls=%async_computation.1 | async-start | bytes 786432 | tf_op jit(solution)/shard_map/all_to_all | solution.py:69
  22.6 18.3 %all-to-all-start = ((bf16[64,4,768]{2,0,1:T(8,128)(2,1)}), bf16[64,4,768]{2,0,1:T(8,128)(2,1)S(1)}, u32[]{:S(2)}, u32[]{:S(2)}) async-start(bf16[64,4,768]{2,0,1:T(8,128)(2,1)} %fusion.23), calls=%async_computation | async-start | bytes 786432 | tf_op jit(solution)/shard_map/all_to_all | solution.py:67
  40.9 10.9 %all-to-all-start.2 = ((bf16[64,4,768]{2,0,1:T(8,128)(2,1)}), bf16[64,4,768]{2,0,1:T(8,128)(2,1)S(1)}, u32[]{:S(2)}, u32[]{:S(2)}) async-start(bf16[64,4,768]{2,0,1:T(8,128)(2,1)} %copy.28), calls=%async_computation.2 | async-start | bytes 786432 | tf_op jit(solution)/shard_map/all_to_all | solution.py:70
  44.3 44.4 %all-gather.3.cloned.1.call-start = ((), (), s32[]{:S(2)}) async-start(), calls=%async_computation.3 | async-start | bytes 1966080 | tf_op jit(solution)/shard_map/all_gather | solution.py:83
  68.2 120.1 %copy-start.1 = (bf16[1,256,1280]{2,1,0:T(8,128)(2,1)S(1)}, bf16[1,256,1280]{2,1,0:T(8,128)(2,1)}, u32[]{:S(2)}) copy-start(bf16[1,256,1280]{2,1,0:T(8,128)(2,1)} %param.17) | copy-start | bytes 1966084
  68.2 120.1 %copy-start.4 = (f32[1280]{0:T(1024)S(1)}, f32[1280]{0:T(1024)}, u32[]{:S(2)}) copy-start(f32[1280]{0:T(1024)} %param.15) | copy-start | bytes 15364
  68.2 120.1 %copy-start.5 = (f32[1280]{0:T(1024)S(1)}, f32[1280]{0:T(1024)}, u32[]{:S(2)}) copy-start(f32[1280]{0:T(1024)} %param.16) | copy-start | bytes 15364
  68.3 120.1 %all-gather.5.cloned.1.call-start = ((), (), s32[]{:S(2)}) async-start(), calls=%async_computation.4 | async-start | bytes 11796480 | tf_op jit(solution)/shard_map/all_gather | solution.py:86
Sparse Core Ops, SparseCore 0:
  68.4 20.2 all-gather.2
  90.2 98.0 all-gather.4
where the time goes:
time: 203 us; the launch traced here: 202 us
  waiting for transfers between devices  129 us (64%)
  blocking collectives  24 us (12%)
  between operations  13.5 us (7%)
  matrix products  11.5 us (6%)
  starting transfers between devices  11.2 us (6%)
  local copies, waits for them, and re-layouts  9.13 us (4%)
  other arithmetic  4.18 us (2%)
    all_gather x1, waiting for transfers between devices, shards(): lax.all_gather(out_weight, 'blk', axis=0, tiled=True)  99.7 us
    all_gather x1, waiting for transfers between devices, shards(): gathered = lax.all_gather(attended, 'uly', axis=1, tiled=True)  19.7 us
    all_gather x1, blocking collectives, shards(): lax.all_gather(head_key, 'blk', axis=0, tiled=True)  12.5 us
    all_gather x1, blocking collectives, shards(): lax.all_gather(head_value, 'blk', axis=0, tiled=True)  11.4 us
    dot_general x1, matrix products, shards(): jnp.dot(gathered, lax.all_gather(out_weight, 'blk', axis=0, tiled=True),...  6.83 us
    all_to_all x1, waiting for transfers between devices, shards(): lax.all_to_all(local_key, 'uly', split_axis=1, concat_axis=0, tiled=True)  5.84 us
    all_to_all x1, starting transfers between devices, shards(): lax.all_to_all(local_key, 'uly', split_axis=1, concat_axis=0, tiled=True)  4.24 us
  transfers between devices with their start and end apart: 5, of which 4 were waited for; matrix products, arithmetic and copies ran while one was open for 4% of the time, Pallas kernels for 0%

commit v1 on v0

--- a/solution.py
+++ b/solution.py
@@ -1,12 +1,315 @@
+import functools
+
 import jax
 import jax.numpy as jnp
 from jax import lax
+from jax.experimental import pallas as pl
+from jax.experimental.pallas import tpu as pltpu
 from jax.sharding import PartitionSpec as P
 
 HEAD = 128
-
-
 EPS = 1e-06
+MESH = pl.DeviceIdType.MESH
+LOG2E = 1.4426950408889634
+
+
+def normalize_rows(rows_ref, gain_ref):
+    count = rows_ref.shape[0]
+    step = 16
+
+    def visit(i, carry):
+        at = pl.ds(pl.multiple_of(i * step, step), step)
+        wide = rows_ref[at, :].astype(jnp.float32)
+        factor = lax.rsqrt(jnp.mean(wide * wide, axis=-1, keepdims=True) + EPS)
+        rows_ref[at, :] = (wide * factor * gain_ref[...]).astype(jnp.bfloat16)
+        return carry
+
+    lax.fori_loop(0, count // step, visit, 0)
+
+
+def fused_kernel(
+    n_u,
+    q_hbm, k_hbm, v_hbm, nq_hbm, nk_hbm, w_hbm, bias_hbm, gate_hbm, res_hbm,
+    out_hbm,
+    q_in, k_in, nq, nk, w, bias, gate, res,
+    q_all, k_all, v_all, att, acc, sent, received, result,
+    load_sem, own_sem, out_sem, send_sem, recv_sem, att_send, att_recv, fwd_send, fwd_recv, sum_send, sum_recv,
+):
+    u = lax.axis_index("uly")
+    b = lax.axis_index("blk")
+    other = 1 - b
+    rows = q_in.shape[0]
+    wide = q_all.shape[1]
+    heads = wide // HEAD
+    block = rows * n_u
+    columns = w.shape[1]
+    tile = 256 if columns % 256 == 0 else 128
+    tiles = columns // tile
+    sibling = u + 1 - 2 * lax.rem(u, 2)
+
+    peers = [(1, du) for du in range(n_u)] + [(0, du) for du in range(1, n_u)]
+
+    def peer_id(db, du):
+        return {"uly": lax.rem(u + du, n_u), "blk": other if db else b}
+
+    barrier = pltpu.get_barrier_semaphore()
+    for db, du in peers:
+        pl.semaphore_signal(barrier, inc=1, device_id=peer_id(db, du), device_id_type=MESH)
+
+    loads = [
+        pltpu.make_async_copy(source, target, load_sem.at[i])
+        for i, (source, target) in enumerate(
+            (
+                (k_hbm.at[0], k_in),
+                (nk_hbm, nk),
+                (q_hbm.at[0], q_in),
+                (nq_hbm, nq),
+                (w_hbm, w),
+                (bias_hbm, bias),
+                (gate_hbm, gate),
+                (res_hbm.at[0], res),
+            )
+        )
+    ]
+    for load in loads[:4]:
+        load.start()
+
+    def spread(index, source, target):
+        copies = []
+        for db, du in peers:
+            to = peer_id(db, du)
+            start = pl.multiple_of((to["blk"] * n_u + to["uly"]) * wide, HEAD)
+            at = pl.multiple_of((0 if db else block) + u * rows, rows)
+            copy = pltpu.make_async_remote_copy(
+                src_ref=source.at[:, pl.ds(start, wide)],
+                dst_ref=target.at[pl.ds(at, rows), :],
+                send_sem=send_sem.at[index, db * n_u + du],
+                recv_sem=recv_sem.at[index, db * n_u + du],
+                device_id=to,
+                device_id_type=MESH,
+            )
+            copy.start()
+            copies.append(copy)
+        mine = pltpu.make_async_copy(
+            source.at[:, pl.ds(pl.multiple_of((b * n_u + u) * wide, HEAD), wide)],
+            target.at[pl.ds(pl.multiple_of(block + u * rows, rows), rows), :],
+            own_sem.at[index],
+        )
+        mine.start()
+        return copies, mine
+
+    pl.semaphore_wait(barrier, len(peers))
+    v_copies, v_mine = spread(0, v_hbm.at[0], v_all)
+    loads[0].wait()
+    loads[1].wait()
+    normalize_rows(k_in, nk)
+    k_copies, k_mine = spread(1, k_in, k_all)
+    loads[2].wait()
+    loads[3].wait()
+    normalize_rows(q_in, nq)
+    q_copies, q_mine = spread(2, q_in, q_all)
+    for load in loads[4:]:
+        load.start()
+
+    for copy in v_copies + k_copies + q_copies[:n_u]:
+        copy.wait_recv()
+    v_mine.wait()
+    k_mine.wait()
+
+    scale = HEAD ** (-0.5) * LOG2E
+
+    def attend(slot, h):
+        feature = pl.ds(h * HEAD, HEAD)
+        scores = lax.dot_general(
+            q_all[pl.ds(slot * block, block), feature],
+            k_all[:, feature],
+            (((1,), (1,)), ((), ())),
+            preferred_element_type=jnp.float32,
+        )
+        peak = jnp.max(scores, axis=1, keepdims=True)
+        weights = jnp.exp2((scores - peak) * scale)
+        total = jnp.sum(weights, axis=1, keepdims=True)
+        numer = jnp.dot(weights.astype(jnp.bfloat16), v_all[:, feature], preferred_element_type=jnp.float32)
+        at = pl.multiple_of(u * wide + h * HEAD, HEAD)
+        att[pl.ds(slot * block, block), pl.ds(at, HEAD)] = (numer / total).astype(jnp.bfloat16)
+
+    chips = n_u // 2
+    pair = [2 * i for i in range(1, chips)]
+
+    def share(slot, h):
+        at = pl.multiple_of(u * wide + h * HEAD, HEAD)
+        place = att.at[pl.ds(slot * block, block), pl.ds(at, HEAD)]
+        copies = []
+        for i, du in enumerate(pair + [None]):
+            to = {"uly": sibling if du is None else lax.rem(u + du, n_u)}
+            copy = pltpu.make_async_remote_copy(
+                src_ref=place,
+                dst_ref=place,
+                send_sem=att_send.at[slot, h, i],
+                recv_sem=att_recv.at[slot, h, i],
+                device_id=to,
+                device_id_type=MESH,
+            )
+            copy.start()
+            copies.append(copy)
+        return copies
+
+    def forward(slot, h, shared):
+        copies = []
+        for i, du in enumerate(pair):
+            shared[i].wait_recv()
+            origin = lax.rem(u + n_u - du, n_u)
+            at = pl.multiple_of(origin * wide + h * HEAD, HEAD)
+            place = att.at[pl.ds(slot * block, block), pl.ds(at, HEAD)]
+            copy = pltpu.make_async_remote_copy(
+                src_ref=place,
+                dst_ref=place,
+                send_sem=fwd_send.at[slot, h, i],
+                recv_sem=fwd_recv.at[slot, h, i],
+                device_id={"uly": sibling},
+                device_id_type=MESH,
+            )
+            copy.start()
+            copies.append(copy)
+        return copies
+
+    shared, forwarded = {}, {}
+    for h in range(heads):
+        attend(0, h)
+        shared[0, h] = share(0, h)
+    for copy in q_copies[n_u:]:
+        copy.wait_recv()
+    q_mine.wait()
+    for h in range(heads):
+        attend(1, h)
+        shared[1, h] = share(1, h)
+
+    for load in loads[4:]:
+        load.wait()
+
+    def gathered(slot):
+        for h in range(heads):
+            forwarded[slot, h] = forward(slot, h, shared[slot, h])
+        for h in range(heads):
+            shared[slot, h][-1].wait_recv()
+        for h in range(heads):
+            for copy in forwarded[slot, h]:
+                copy.wait_recv()
+
+    def sum_copy(j):
+        at = pl.ds(pl.multiple_of(j * tile, tile), tile)
+        return pltpu.make_async_remote_copy(
+            src_ref=sent.at[:, at],
+            dst_ref=received.at[:, at],
+            send_sem=sum_send.at[j],
+            recv_sem=sum_recv.at[j],
+            device_id={"blk": other},
+            device_id_type=MESH,
+        )
+
+    def out_copy(j):
+        at = pl.ds(pl.multiple_of(j * tile, tile), tile)
+        return pltpu.make_async_copy(result.at[:, at], out_hbm.at[0, :, at], out_sem.at[j])
+
+    gathered(0)
+
+    def project_other(j, carry):
+        at = pl.ds(pl.multiple_of(j * tile, tile), tile)
+        product = jnp.dot(att[:block, :], w[:, at], preferred_element_type=jnp.float32)
+        sent[:, at] = product.astype(jnp.bfloat16)
+        sum_copy(j).start()
+        return carry
+
+    lax.fori_loop(0, tiles, project_other, 0)
+
+    gathered(1)
+
+    def project_own(j, carry):
+        at = pl.ds(pl.multiple_of(j * tile, tile), tile)
+        product = jnp.dot(att[block:, :], w[:, at], preferred_element_type=jnp.float32)
+        acc[:, at] = res[:, at].astype(jnp.float32) + gate[:, at] * (product + bias[:, at])
+        return carry
+
+    lax.fori_loop(0, tiles, project_own, 0)
+
+    def finish(j, carry):
+        at = pl.ds(pl.multiple_of(j * tile, tile), tile)
+        sum_copy(j).wait_recv()
+        result[:, at] = (acc[:, at] + gate[:, at] * received[:, at].astype(jnp.float32)).astype(jnp.bfloat16)
+        out_copy(j).start()
+        return carry
+
+    lax.fori_loop(0, tiles, finish, 0)
+
+    for copy in v_copies + k_copies + q_copies:
+        copy.wait_send()
+    for copies in list(shared.values()) + list(forwarded.values()):
+        for copy in copies:
+            copy.wait_send()
+
+    def drain(j, carry):
+        sum_copy(j).wait_send()
+        out_copy(j).wait()
+        return carry
+
+    lax.fori_loop(0, tiles, drain, 0)
+
+
+def fused_shards(n_u, n_b, q, k, v, norm_query, norm_key, out_weight, out_bias, gate, residual):
+    rows, features = q.shape[1:]
+    depth, columns = out_weight.shape
+    wide = features // (n_u * n_b)
+    heads = wide // HEAD
+    block = rows * n_u
+    seq = block * n_b
+    tiles = columns // (256 if columns % 256 == 0 else 128)
+    chips = n_u // 2
+    bf16, f32 = jnp.bfloat16, jnp.float32
+    dma = pltpu.SemaphoreType.DMA
+    return pl.pallas_call(
+        functools.partial(fused_kernel, n_u),
+        out_shape=jax.ShapeDtypeStruct(residual.shape, bf16),
+        in_specs=[pl.BlockSpec(memory_space=pl.ANY)] * 9,
+        out_specs=pl.BlockSpec(memory_space=pl.ANY),
+        scratch_shapes=[
+            pltpu.VMEM((rows, features), bf16),
+            pltpu.VMEM((rows, features), bf16),
+            pltpu.VMEM((1, features), f32),
+            pltpu.VMEM((1, features), f32),
+            pltpu.VMEM((depth, columns), bf16),
+            pltpu.VMEM((1, columns), f32),
+            pltpu.VMEM((1, columns), f32),
+            pltpu.VMEM((block, columns), bf16),
+            pltpu.VMEM((seq, wide), bf16),
+            pltpu.VMEM((seq, wide), bf16),
+            pltpu.VMEM((seq, wide), bf16),
+            pltpu.VMEM((seq, depth), bf16),
+            pltpu.VMEM((block, columns), f32),
+            pltpu.VMEM((block, columns), bf16),
+            pltpu.VMEM((block, columns), bf16),
+            pltpu.VMEM((block, columns), bf16),
+            dma((8,)),
+            dma((3,)),
+            dma((tiles,)),
+            dma((3, 2 * n_u)),
+            dma((3, 2 * n_u)),
+            dma((2, heads, chips)),
+            dma((2, heads, chips)),
+            dma((2, heads, max(chips - 1, 1))),
+            dma((2, heads, max(chips - 1, 1))),
+            dma((tiles,)),
+            dma((tiles,)),
+        ],
+        compiler_params=pltpu.CompilerParams(
+            collective_id=0, has_side_effects=True, vmem_limit_bytes=48 * 1024 * 1024
+        ),
+    )(
+        q, k, v,
+        norm_query.reshape(1, features), norm_key.reshape(1, features),
+        out_weight,
+        out_bias.reshape(1, columns), gate.reshape(1, columns),
+        residual,
+    )
 
 
 def normalize(rows_in, gain):
@@ -44,7 +347,7 @@
     return (new_peak, total, accum)
 
 
-def attend(state, keys, values, queries):
+def attend_blocks(state, keys, values, queries):
     length = keys.shape[0]
     stride = 512
     count = keys.shape[1] // HEAD
@@ -58,7 +361,7 @@
     return state
 
 
-def shards(
+def general_shards(
     query_rows, key_rows, value_rows, norm_query, norm_key, out_weight, out_bias, gate, residual
 ):
     local_query = normalize(query_rows[0], norm_query)
@@ -70,7 +373,7 @@
         lax.all_to_all(local_value, "uly", split_axis=1, concat_axis=0, tiled=True),
     )
     queries = split_heads(head_query)
-    state = attend(
+    state = attend_blocks(
         initial_state(queries),
         lax.all_gather(head_key, "blk", axis=0, tiled=True),
         lax.all_gather(head_value, "blk", axis=0, tiled=True),
@@ -91,6 +394,7 @@
 
 
 def solution(mesh):
+    n_u, n_b = mesh.shape["uly"], mesh.shape["blk"]
     placed = (
         P(("dp", "blk"), "uly", None),
         P(("dp", "blk"), "uly", None),
@@ -102,6 +406,13 @@
         P("uly"),
         P(("dp", "blk"), None, "uly"),
     )
+
+    def shards(query_rows, *rest):
+        heads = query_rows.shape[2] // HEAD
+        if n_b == 2 and n_u % 2 == 0 and heads % (n_u * n_b) == 0:
+            return fused_shards(n_u, n_b, query_rows, *rest)
+        return general_shards(query_rows, *rest)
+
     return jax.shard_map(
         shards, mesh=mesh, in_specs=placed, out_specs=P(("dp", "blk"), None, "uly"), check_vma=False
     )

time: 203 us -> 51.9 us (0.26)
  waiting for transfers between devices: 129 us -> 0 us
  Pallas kernels: 0 us -> 43.7 us
  blocking collectives: 24 us -> 0 us
  between operations: 13.5 us -> 0.02 us
  matrix products: 11.5 us -> 0 us
  starting transfers between devices: 11.2 us -> 0 us
  other arithmetic: 4.18 us -> 0 us
    all_gather x2 -> x0, waiting for transfers between devices: 119 us -> none  [the longest x1 99.7 us: shards(): lax.all_gather(out_weight, 'blk', axis=0, tiled=True)]
    pallas_call x0 -> x1, Pallas kernels: none -> 43.7 us  [fused_shards(): pl.pallas_call(functools.partial(fused_kernel, n_u), out_shape=jax.ShapeD...]
    all_gather x2 -> x0, blocking collectives: 24 us -> none  [the longest x1 12.5 us: shards(): lax.all_gather(head_key, 'blk', axis=0, tiled=True)]
    dot_general x3 -> x0, matrix products: 11.5 us -> none  [the longest x1 6.83 us: shards(): jnp.dot(gathered, lax.all_gather(out_weight, 'blk', axis=0, tiled=True),...]
    all_to_all x3 -> x0, starting transfers between devices: 11.2 us -> none  [the longest x1 4.24 us: shards(): lax.all_to_all(local_key, 'uly', split_axis=1, concat_axis=0, tiled=True)]
    all_to_all x3 -> x0, waiting for transfers between devices: 8.45 us -> none  [the longest x1 5.84 us: shards(): lax.all_to_all(local_key, 'uly', split_axis=1, concat_axis=0, tiled=True)]
    unnamed x12 -> x13, local copies, waits for them, and re-layouts: 0.02 us -> 6.32 us
    all_gather x2 -> x0, local copies, waits for them, and re-layouts: 3.47 us -> none  [the longest x1 2.3 us: shards(): lax.all_gather(head_value, 'blk', axis=0, tiled=True)]
  transfers between devices with their start and end apart: 5 -> 0, of which waited for: 4 -> 0; matrix products, arithmetic and copies ran while one was open for 4% -> 0% of each run, Pallas kernels for 0% -> 0%
where the time goes in v1:
time: 51.9 us; the launch traced here: 51.5 us
  Pallas kernels  43.7 us (84%)
  local copies, waits for them, and re-layouts  7.73 us (15%)
    pallas_call x1, Pallas kernels, fused_shards(): pl.pallas_call(functools.partial(fused_kernel, n_u), out_shape=jax.ShapeD...  43.7 us
    unnamed x13, local copies, waits for them, and re-layouts  6.32 us

profile of v1, /device:TPU:0, one launch (start us, length us, event | category | flops | bytes accessed | tf_op | source)
XLA Modules:
  0.0 51.5 jit_solution(957310230100381185)
XLA Ops:
  0.0 0.7 %reshape.14.bias_hbm = f32[1,1280]{1,0:T(1,128)S(1)} reshape(f32[1280]{0:T(1024)} %param.15) | data formatting | bytes 10240 | tf_op jit(solution)/shard_map/reshape | solution.py:310
  0.7 0.7 %reshape.15.gate_hbm = f32[1,1280]{1,0:T(1,128)S(1)} reshape(f32[1280]{0:T(1024)} %param.16) | data formatting | bytes 10240 | tf_op jit(solution)/shard_map/reshape | solution.py:310
  1.4 0.0 copy-start
  1.4 1.1 %copy-done = bf16[1,256,1280]{2,1,0:T(8,128)(2,1)S(1)} copy-done((bf16[1,256,1280]{2,1,0:T(8,128)(2,1)S(1)}, bf16[1,256,1280]{2,1,0:T(8,128)(2,1)}, u32[]{:S(2)}) %copy-start) | copy-done | bytes 655384
  2.5 0.0 copy-start.1
  2.5 1.0 %copy-done.1 = bf16[1,64,3072]{2,1,0:T(8,128)(2,1)S(1)} copy-done((bf16[1,64,3072]{2,1,0:T(8,128)(2,1)S(1)}, bf16[1,64,3072]{2,1,0:T(8,128)(2,1)}, u32[]{:S(2)}) %copy-start.1) | copy-done | bytes 393240
  3.5 0.0 copy-start.2
  3.5 1.0 %copy-done.2 = bf16[1,64,3072]{2,1,0:T(8,128)(2,1)S(1)} copy-done((bf16[1,64,3072]{2,1,0:T(8,128)(2,1)S(1)}, bf16[1,64,3072]{2,1,0:T(8,128)(2,1)}, u32[]{:S(2)}) %copy-start.2) | copy-done | bytes 393240
  4.5 0.0 copy-start.3
  4.5 1.0 %copy-done.3 = bf16[1,64,3072]{2,1,0:T(8,128)(2,1)S(1)} copy-done((bf16[1,64,3072]{2,1,0:T(8,128)(2,1)S(1)}, bf16[1,64,3072]{2,1,0:T(8,128)(2,1)}, u32[]{:S(2)}) %copy-start.3) | copy-done | bytes 393240
  5.5 0.0 copy-start.4
  5.5 0.7 %copy-done.4 = f32[3072]{0:T(1024)S(1)} copy-done((f32[3072]{0:T(1024)S(1)}, f32[3072]{0:T(1024)}, u32[]{:S(2)}) %copy-start.4) | copy-done | bytes 12312
  6.2 0.0 copy-start.5
  6.2 0.7 %copy-done.5 = f32[3072]{0:T(1024)S(1)} copy-done((f32[3072]{0:T(1024)S(1)}, f32[3072]{0:T(1024)}, u32[]{:S(2)}) %copy-start.5) | copy-done | bytes 12312
  6.9 43.7 %shard_map.91 = bf16[1,256,1280]{2,1,0:T(8,128)(2,1)S(1)} custom-call(bf16[1,64,3072]{2,1,0:T(8,128)(2,1)S(1)} %copy-done.1, bf16[1,64,3072]{2,1,0:T(8,128)(2,1)S(1)} %copy-done.2, bf16[1,64,3072]{2,1,0:T(8,128)(2,1)S(1)} %copy-done.3, f32[1,3072]{1,0:T(1,128)S(1)} %bitcast.2, f32[1,3072]{1,0:T(1,128)S(1)} %bitcast.3, bf16[1536,1280]{1,0:T(8,128)(2,1)} %w_hbm.1, ...), custom_call_target="tpu_custom_call" | custom-call | tf_op jit(solution)/shard_map/pallas_call | solution.py:269
  50.6 0.8 %copy.11 = bf16[1,256,1280]{2,1,0:T(8,128)(2,1)} copy(bf16[1,256,1280]{2,1,0:T(8,128)(2,1)S(1)} %shard_map.91) | data formatting | bytes 1310720
Async XLA Ops:
  1.4 1.1 %copy-start = (bf16[1,256,1280]{2,1,0:T(8,128)(2,1)S(1)}, bf16[1,256,1280]{2,1,0:T(8,128)(2,1)}, u32[]{:S(2)}) copy-start(bf16[1,256,1280]{2,1,0:T(8,128)(2,1)} %res_hbm.1) | copy-start | bytes 1966084
  2.5 1.0 %copy-start.1 = (bf16[1,64,3072]{2,1,0:T(8,128)(2,1)S(1)}, bf16[1,64,3072]{2,1,0:T(8,128)(2,1)}, u32[]{:S(2)}) copy-start(bf16[1,64,3072]{2,1,0:T(8,128)(2,1)} %q_hbm.1) | copy-start | bytes 1179652
  3.5 1.0 %copy-start.2 = (bf16[1,64,3072]{2,1,0:T(8,128)(2,1)S(1)}, bf16[1,64,3072]{2,1,0:T(8,128)(2,1)}, u32[]{:S(2)}) copy-start(bf16[1,64,3072]{2,1,0:T(8,128)(2,1)} %k_hbm.1) | copy-start | bytes 1179652
  4.5 1.0 %copy-start.3 = (bf16[1,64,3072]{2,1,0:T(8,128)(2,1)S(1)}, bf16[1,64,3072]{2,1,0:T(8,128)(2,1)}, u32[]{:S(2)}) copy-start(bf16[1,64,3072]{2,1,0:T(8,128)(2,1)} %v_hbm.1) | copy-start | bytes 1179652
  5.5 0.7 %copy-start.4 = (f32[3072]{0:T(1024)S(1)}, f32[3072]{0:T(1024)}, u32[]{:S(2)}) copy-start(f32[3072]{0:T(1024)} %param.12) | copy-start | bytes 36868
  6.2 0.7 %copy-start.5 = (f32[3072]{0:T(1024)S(1)}, f32[3072]{0:T(1024)}, u32[]{:S(2)}) copy-start(f32[3072]{0:T(1024)} %param.13) | copy-start | bytes 36868

commit v2 on v1

v2 whole, which is shorter than its diff:
```python
import functools

import jax
import jax.numpy as jnp
from jax import lax
from jax.experimental import pallas as pl
from jax.experimental.pallas import tpu as pltpu
from jax.sharding import PartitionSpec as P

HEAD = 128
EPS = 1e-06
MESH = pl.DeviceIdType.MESH
LOG2E = 1.4426950408889634


def normalize_rows(rows_ref, gain_ref):
    count = rows_ref.shape[0]
    step = 16

    def visit(i, carry):
        at = pl.ds(pl.multiple_of(i * step, step), step)
        wide = rows_ref[at, :].astype(jnp.float32)
        factor = lax.rsqrt(jnp.mean(wide * wide, axis=-1, keepdims=True) + EPS)
        rows_ref[at, :] = (wide * factor * gain_ref[...]).astype(jnp.bfloat16)
        return carry

    lax.fori_loop(0, count // step, visit, 0)


def fused_kernel(
    n_u, parts,
    q_hbm, k_hbm, v_hbm, nq_hbm, nk_hbm, w_hbm, bias_hbm, gate_hbm, res_hbm,
    out_hbm,
    q_in, k_in, nq, nk, w, bias_line, gate_line, res, bias, gate,
    q_all, k_all, v_all, att, acc, sent, received, result,
    load_sem, own_sem, out_sem, send_sem, recv_sem, q_send, q_recv, att_send, att_recv, fwd_send, fwd_recv, sum_send, sum_recv,
):
    u = lax.axis_index("uly")
    b = lax.axis_index("blk")
    other = 1 - b
    rows = q_in.shape[0]
    wide = q_all.shape[1]
    heads = wide // HEAD
    block = rows * n_u
    columns = w.shape[1]
    tile = 256 if columns % 256 == 0 else 128
    tiles = columns // tile
    sibling = u + 1 - 2 * lax.rem(u, 2)

    peers = [(1, du) for du in range(n_u)] + [(0, du) for du in range(1, n_u)]

    def peer_id(db, du):
        return {"uly": lax.rem(u + du, n_u), "blk": other if db else b}

    barrier = pltpu.get_barrier_semaphore()
    for db, du in peers:
        pl.semaphore_signal(barrier, inc=1, device_id=peer_id(db, du), device_id_type=MESH)

    loads = [
        pltpu.make_async_copy(source, target, load_sem.at[i])
        for i, (source, target) in enumerate(
            (
                (k_hbm.at[0], k_in),
                (nk_hbm, nk),
                (q_hbm.at[0], q_in),
                (nq_hbm, nq),
                (w_hbm, w),
                (bias_hbm, bias_line),
                (gate_hbm, gate_line),
                (res_hbm.at[0], res),
            )
        )
    ]
    for load in loads[:4]:
        load.start()

    def place_copy(source, target, db, du, first, count, at, send, recv):
        to = peer_id(db, du)
        start = pl.multiple_of((to["blk"] * n_u + to["uly"]) * wide, HEAD)
        copy = pltpu.make_async_remote_copy(
            src_ref=source.at[pl.ds(first, count), pl.ds(start, wide)],
            dst_ref=target.at[pl.ds(at, count), :],
            send_sem=send,
            recv_sem=recv,
            device_id=to,
            device_id_type=MESH,
        )
        copy.start()
        return copy

    def keep(index, source, target):
        copy = pltpu.make_async_copy(
            source.at[:, pl.ds(pl.multiple_of((b * n_u + u) * wide, HEAD), wide)],
            target.at[pl.ds(pl.multiple_of(block + u * rows, rows), rows), :],
            own_sem.at[index],
        )
        copy.start()
        return copy

    def spread(index, source, target, some):
        return [
            place_copy(
                source, target, db, du, 0, rows, pl.multiple_of((0 if db else block) + u * rows, rows),
                send_sem.at[index, db * n_u + du], recv_sem.at[index, db * n_u + du],
            )
            for db, du in some
        ]

    piece = rows // parts
    span = piece * n_u

    def spread_part(c):
        return [
            place_copy(
                q_in, q_all, 1, du, c * piece, piece, pl.multiple_of(c * span + u * piece, piece),
                q_send.at[c, du], q_recv.at[c, du],
            )
            for du in range(n_u)
        ]

    pl.semaphore_wait(barrier, len(peers))
    v_copies = spread(0, v_hbm.at[0], v_all, peers)
    v_mine = keep(0, v_hbm.at[0], v_all)
    loads[0].wait()
    loads[1].wait()
    normalize_rows(k_in, nk)
    k_copies = spread(1, k_in, k_all, peers)
    k_mine = keep(1, k_in, k_all)
    loads[2].wait()
    loads[3].wait()
    normalize_rows(q_in, nq)
    part_copies = [spread_part(0)]
    for load in loads[4:]:
        load.start()

    for copy in v_copies + k_copies:
        copy.wait_recv()
    v_mine.wait()
    k_mine.wait()
    for c in range(1, parts):
        part_copies.append(spread_part(c))
    q_copies = spread(2, q_in, q_all, peers[n_u:])
    q_mine = keep(2, q_in, q_all)

    scale = HEAD ** (-0.5) * LOG2E
    sections = [(c * span, span) for c in range(parts)] + [(block, block)]

    def attend(section):
        first, count = sections[section]
        for h in range(heads):
            feature = pl.ds(h * HEAD, HEAD)
            scores = lax.dot_general(
                q_all[pl.ds(first, count), feature],
                k_all[:, feature],
                (((1,), (1,)), ((), ())),
                preferred_element_type=jnp.float32,
            )
            peak = jnp.max(scores, axis=1, keepdims=True)
            weights = jnp.exp2((scores - peak) * scale)
            total = jnp.sum(weights, axis=1, keepdims=True)
            numer = jnp.dot(weights.astype(jnp.bfloat16), v_all[:, feature], preferred_element_type=jnp.float32)
            at = pl.multiple_of(u * wide + h * HEAD, HEAD)
            att[pl.ds(first, count), pl.ds(at, HEAD)] = (numer / total).astype(jnp.bfloat16)

    chips = n_u // 2
    pair = [2 * i for i in range(1, chips)]
    shared, forwarded = {}, {}

    def pass_on(section, origin, to, send, recv):
        first, count = sections[section]
        place = att.at[pl.ds(first, count), pl.ds(pl.multiple_of(origin * wide, HEAD), wide)]
        copy = pltpu.make_async_remote_copy(
            src_ref=place, dst_ref=place, send_sem=send, recv_sem=recv, device_id={"uly": to}, device_id_type=MESH
        )
        copy.start()
        return copy

    def share(section):
        shared[section] = [
            pass_on(section, u, to, att_send.at[section, i], att_recv.at[section, i])
            for i, to in enumerate([lax.rem(u + du, n_u) for du in pair] + [sibling])
        ]

    def gather(section):
        forwarded[section] = []
        for i, du in enumerate(pair):
            shared[section][i].wait_recv()
            origin = lax.rem(u + n_u - du, n_u)
            forwarded[section].append(
                pass_on(section, origin, sibling, fwd_send.at[section, i], fwd_recv.at[section, i])
            )
        shared[section][-1].wait_recv()
        for copy in forwarded[section]:
            copy.wait_recv()

    def columns_of(j):
        return pl.ds(pl.multiple_of(j * tile, tile), tile)

    def sum_copy(c, j):
        place = (pl.ds(c * span, span), columns_of(j))
        return pltpu.make_async_remote_copy(
            src_ref=sent.at[place],
            dst_ref=received.at[place],
            send_sem=sum_send.at[c, j],
            recv_sem=sum_recv.at[c, j],
            device_id={"blk": other},
            device_id_type=MESH,
        )

    def out_copy(j):
        return pltpu.make_async_copy(result.at[:, columns_of(j)], out_hbm.at[0, :, columns_of(j)], out_sem.at[j])

    def project_part(c):
        def visit(j, carry):
            product = jnp.dot(
                att[pl.ds(c * span, span), :], w[:, columns_of(j)], preferred_element_type=jnp.float32
            )
            sent[pl.ds(c * span, span), columns_of(j)] = product.astype(jnp.bfloat16)
            sum_copy(c, j).start()
            return carry

        lax.fori_loop(0, tiles, visit, 0)

    def attend_own():
        for copy in q_copies:
            copy.wait_recv()
        q_mine.wait()
        attend(parts)
        share(parts)

    for c in range(parts):
        for copy in part_copies[c]:
            copy.wait_recv()
        attend(c)
        share(c)

    for load in loads[4:]:
        load.wait()
    bias[...] = bias_line[...].reshape(1, columns)
    gate[...] = gate_line[...].reshape(1, columns)

    for c in range(parts):
        gather(c)
        project_part(c)
        if c == 0:
            attend_own()
    gather(parts)

    def project_own(j, carry):
        at = columns_of(j)
        product = jnp.dot(att[block:, :], w[:, at], preferred_element_type=jnp.float32)
        acc[:, at] = res[:, at].astype(jnp.float32) + gate[:, at] * (product + bias[:, at])
        return carry

    lax.fori_loop(0, tiles, project_own, 0)

    def finish(j, carry):
        at = columns_of(j)
        for c in range(parts):
            sum_copy(c, j).wait_recv()
        for c in range(parts):
            for origin in range(n_u):
                here = pl.ds(origin * rows + c * piece, piece)
                there = pl.ds(c * span + origin * piece, piece)
                mixed = acc[here, at] + gate[:, at] * received[there, at].astype(jnp.float32)
                result[here, at] = mixed.astype(jnp.bfloat16)
        out_copy(j).start()
        return carry

    lax.fori_loop(0, tiles, finish, 0)

    for copy in v_copies + k_copies + q_copies:
        copy.wait_send()
    for copies in part_copies + list(shared.values()) + list(forwarded.values()):
        for copy in copies:
            copy.wait_send()

    def drain(j, carry):
        for c in range(parts):
            sum_copy(c, j).wait_send()
        out_copy(j).wait()
        return carry

    lax.fori_loop(0, tiles, drain, 0)


def fused_shards(n_u, n_b, q, k, v, norm_query, norm_key, out_weight, out_bias, gate, residual):
    rows, features = q.shape[1:]
    depth, columns = out_weight.shape
    wide = features // (n_u * n_b)
    heads = wide // HEAD
    block = rows * n_u
    seq = block * n_b
    tiles = columns // (256 if columns % 256 == 0 else 128)
    chips = n_u // 2
    parts = 2
    bf16, f32 = jnp.bfloat16, jnp.float32
    dma = pltpu.SemaphoreType.DMA
    return pl.pallas_call(
        functools.partial(fused_kernel, n_u, parts),
        out_shape=jax.ShapeDtypeStruct(residual.shape, bf16),
        in_specs=[pl.BlockSpec(memory_space=pl.ANY)] * 9,
        out_specs=pl.BlockSpec(memory_space=pl.ANY),
        scratch_shapes=[
            pltpu.VMEM((rows, features), bf16),
            pltpu.VMEM((rows, features), bf16),
            pltpu.VMEM((1, features), f32),
            pltpu.VMEM((1, features), f32),
            pltpu.VMEM((depth, columns), bf16),
            pltpu.VMEM((columns,), f32),
            pltpu.VMEM((columns,), f32),
            pltpu.VMEM((block, columns), bf16),
            pltpu.VMEM((1, columns), f32),
            pltpu.VMEM((1, columns), f32),
            pltpu.VMEM((seq, wide), bf16),
            pltpu.VMEM((seq, wide), bf16),
            pltpu.VMEM((seq, wide), bf16),
            pltpu.VMEM((seq, depth), bf16),
            pltpu.VMEM((block, columns), f32),
            pltpu.VMEM((block, columns), bf16),
            pltpu.VMEM((block, columns), bf16),
            pltpu.VMEM((block, columns), bf16),
            dma((8,)),
            dma((3,)),
            dma((tiles,)),
            dma((3, 2 * n_u)),
            dma((3, 2 * n_u)),
            dma((parts, n_u)),
            dma((parts, n_u)),
            dma((parts + 1, chips)),
            dma((parts + 1, chips)),
            dma((parts + 1, max(chips - 1, 1))),
            dma((parts + 1, max(chips - 1, 1))),
            dma((parts, tiles)),
            dma((parts, tiles)),
        ],
        compiler_params=pltpu.CompilerParams(
            collective_id=0, has_side_effects=True, vmem_limit_bytes=63 * 1024 * 1024
        ),
    )(
        q, k, v,
        norm_query.reshape(1, features), norm_key.reshape(1, features),
        out_weight,
        out_bias, gate,
        residual,
    )


def normalize(rows_in, gain):
    wide = rows_in.astype(jnp.float32)
    factor = lax.rsqrt(jnp.mean(wide * wide, axis=-1, keepdims=True) + EPS)
    return (wide * factor * gain).astype(jnp.bfloat16)


def split_heads(array):
    return array.reshape(array.shape[0], array.shape[1] // HEAD, HEAD)


def initial_state(queries):
    count = queries.shape[1]
    length = queries.shape[0]
    return (
        jnp.full((count, length), -1e30, jnp.float32),
        jnp.zeros((count, length), jnp.float32),
        jnp.zeros((count, length, HEAD), jnp.float32),
    )


def absorb(state, keys, values, queries):
    peak, total, accum = state
    scores = jnp.einsum(
        "qhd,khd->hqk", queries, keys, preferred_element_type=jnp.float32
    ) * HEAD ** (-0.5)
    new_peak = jnp.maximum(peak, jnp.max(scores, axis=2))
    factor = jnp.exp(peak - new_peak)
    weights = jnp.exp(scores - new_peak[:, :, None])
    total = total * factor + jnp.sum(weights, axis=2)
    accum = accum * factor[:, :, None] + jnp.einsum(
        "hqk,khd->hqd", weights.astype(jnp.bfloat16), values, preferred_element_type=jnp.float32
    )
    return (new_peak, total, accum)


def attend_blocks(state, keys, values, queries):
    length = keys.shape[0]
    stride = 512
    count = keys.shape[1] // HEAD
    key_blocks = keys.reshape(length // stride, stride, count, HEAD)
    value_blocks = values.reshape(length // stride, stride, count, HEAD)

    def visit(carry, pair):
        return (absorb(carry, pair[0], pair[1], queries), None)

    state, unused = lax.scan(visit, state, (key_blocks, value_blocks))
    return state


def general_shards(
    query_rows, key_rows, value_rows, norm_query, norm_key, out_weight, out_bias, gate, residual
):
    local_query = normalize(query_rows[0], norm_query)
    local_key = normalize(key_rows[0], norm_key)
    local_value = value_rows[0]
    head_query = lax.all_to_all(local_query, "uly", split_axis=1, concat_axis=0, tiled=True)
    head_key, head_value = (
        lax.all_to_all(local_key, "uly", split_axis=1, concat_axis=0, tiled=True),
        lax.all_to_all(local_value, "uly", split_axis=1, concat_axis=0, tiled=True),
    )
    queries = split_heads(head_query)
    state = attend_blocks(
        initial_state(queries),
        lax.all_gather(head_key, "blk", axis=0, tiled=True),
        lax.all_gather(head_value, "blk", axis=0, tiled=True),
        queries,
    )
    peak, total, accum = state
    length = queries.shape[0]
    attended = (accum / total[:, :, None]).astype(jnp.bfloat16)
    attended = attended.transpose(1, 0, 2).reshape(length, queries.shape[1] * HEAD)
    gathered = lax.all_gather(attended, "uly", axis=1, tiled=True)
    projected = jnp.dot(
        gathered,
        lax.all_gather(out_weight, "blk", axis=0, tiled=True),
        preferred_element_type=jnp.float32,
    )
    mixed = residual[0].astype(jnp.float32) + gate * (projected + out_bias)
    return mixed.astype(jnp.bfloat16)[None]


def solution(mesh):
    n_u, n_b = mesh.shape["uly"], mesh.shape["blk"]
    placed = (
        P(("dp", "blk"), "uly", None),
        P(("dp", "blk"), "uly", None),
        P(("dp", "blk"), "uly", None),
        P(),
        P(),
        P("blk", "uly"),
        P("uly"),
        P("uly"),
        P(("dp", "blk"), None, "uly"),
    )

    def shards(query_rows, *rest):
        heads = query_rows.shape[2] // HEAD
        if n_b == 2 and n_u % 2 == 0 and heads % (n_u * n_b) == 0:
            return fused_shards(n_u, n_b, query_rows, *rest)
        return general_shards(query_rows, *rest)

    return jax.shard_map(
        shards, mesh=mesh, in_specs=placed, out_specs=P(("dp", "blk"), None, "uly"), check_vma=False
    )
```

time: 51.9 us -> 43.4 us (0.84)
  local copies, waits for them, and re-layouts: 7.73 us -> 1.97 us
  Pallas kernels: 43.7 us -> 41.2 us
    unnamed x13 -> x1, local copies, waits for them, and re-layouts: 6.32 us -> 1.97 us
    pallas_call x1, Pallas kernels: 43.7 us -> 41.2 us  [fused_shards(): pl.pallas_call(functools.partial(fused_kernel, n_u, parts), out_shape=jax...]
    reshape x2 -> x0, local copies, waits for them, and re-layouts: 1.4 us -> none  [the longest x1 0.7 us: fused_shards(): gate.reshape(1, columns)]
where the time goes in v2:
time: 43.4 us; the launch traced here: 43.2 us
  Pallas kernels  41.2 us (95%)
  local copies, waits for them, and re-layouts  1.97 us (5%)
    pallas_call x1, Pallas kernels, fused_shards(): pl.pallas_call(functools.partial(fused_kernel, n_u, parts), out_shape=jax...  41.2 us
    unnamed x1, local copies, waits for them, and re-layouts  1.97 us

profile of v2, /device:TPU:0, one launch (start us, length us, event | category | flops | bytes accessed | tf_op | source)
XLA Modules:
  0.0 43.2 jit_solution(3860552420834575106)
XLA Ops:
  0.0 41.2 %shard_map.91 = bf16[1,256,1280]{2,1,0:T(8,128)(2,1)} custom-call(bf16[1,64,3072]{2,1,0:T(8,128)(2,1)} %q_hbm.1, bf16[1,64,3072]{2,1,0:T(8,128)(2,1)} %k_hbm.1, bf16[1,64,3072]{2,1,0:T(8,128)(2,1)} %v_hbm.1, f32[1,3072]{1,0:T(1,128)} %bitcast.2, f32[1,3072]{1,0:T(1,128)} %bitcast.3, bf16[1536,1280]{1,0:T(8,128)(2,1)} %w_hbm.1, f32[1280]{0:T(1024)} %bias_hbm.1, ...), custom_call_target="tpu_custom_call" | custom-call | tf_op jit(solution)/shard_map/pallas_call | solution.py:299
  41.2 2.0 %copy.11 = bf16[1,256,1280]{2,1,0:T(8,128)(2,1)} copy(bf16[1,256,1280]{2,1,0:T(8,128)(2,1)} %shard_map.91) | data formatting | bytes 1310720

commit v3 on v2

--- a/solution.py
+++ b/solution.py
@@ -118,17 +118,17 @@
             for du in range(n_u)
         ]
 
+    loads[0].wait()
+    loads[1].wait()
+    normalize_rows(k_in, nk)
+    loads[2].wait()
+    loads[3].wait()
+    normalize_rows(q_in, nq)
     pl.semaphore_wait(barrier, len(peers))
     v_copies = spread(0, v_hbm.at[0], v_all, peers)
     v_mine = keep(0, v_hbm.at[0], v_all)
-    loads[0].wait()
-    loads[1].wait()
-    normalize_rows(k_in, nk)
     k_copies = spread(1, k_in, k_all, peers)
     k_mine = keep(1, k_in, k_all)
-    loads[2].wait()
-    loads[3].wait()
-    normalize_rows(q_in, nq)
     part_copies = [spread_part(0)]
     for load in loads[4:]:
         load.start()
@@ -139,8 +139,6 @@
     k_mine.wait()
     for c in range(1, parts):
         part_copies.append(spread_part(c))
-    q_copies = spread(2, q_in, q_all, peers[n_u:])
-    q_mine = keep(2, q_in, q_all)
 
     scale = HEAD ** (-0.5) * LOG2E
     sections = [(c * span, span) for c in range(parts)] + [(block, block)]
@@ -234,6 +232,9 @@
         attend(c)
         share(c)
 
+    q_copies = spread(2, q_in, q_all, peers[n_u:])
+    q_mine = keep(2, q_in, q_all)
+
     for load in loads[4:]:
         load.wait()
     bias[...] = bias_line[...].reshape(1, columns)
@@ -242,7 +243,7 @@
     for c in range(parts):
         gather(c)
         project_part(c)
-        if c == 0:
+        if c == parts - 1:
             attend_own()
     gather(parts)
 

time: 43.4 us -> 42.7 us (0.984)
  Pallas kernels: 41.2 us -> 40.6 us
    pallas_call x1, Pallas kernels: 41.2 us -> 40.6 us  [fused_shards(): pl.pallas_call(functools.partial(fused_kernel, n_u, parts), out_shape=jax...]
where the time goes in v3:
time: 42.7 us; the launch traced here: 42.6 us
  Pallas kernels  40.6 us (95%)
  local copies, waits for them, and re-layouts  1.97 us (5%)
    pallas_call x1, Pallas kernels, fused_shards(): pl.pallas_call(functools.partial(fused_kernel, n_u, parts), out_shape=jax...  40.6 us
    unnamed x1, local copies, waits for them, and re-layouts  1.97 us

profile of v3, /device:TPU:0, one launch (start us, length us, event | category | flops | bytes accessed | tf_op | source)
XLA Modules:
  0.0 42.6 jit_solution(16439904047481171340)
XLA Ops:
  0.0 40.6 %shard_map.91 = bf16[1,256,1280]{2,1,0:T(8,128)(2,1)} custom-call(bf16[1,64,3072]{2,1,0:T(8,128)(2,1)} %q_hbm.1, bf16[1,64,3072]{2,1,0:T(8,128)(2,1)} %k_hbm.1, bf16[1,64,3072]{2,1,0:T(8,128)(2,1)} %v_hbm.1, f32[1,3072]{1,0:T(1,128)} %bitcast.2, f32[1,3072]{1,0:T(1,128)} %bitcast.3, bf16[1536,1280]{1,0:T(8,128)(2,1)} %w_hbm.1, f32[1280]{0:T(1024)} %bias_hbm.1, ...), custom_call_target="tpu_custom_call" | custom-call | tf_op jit(solution)/shard_map/pallas_call | solution.py:300
  40.6 2.0 %copy.11 = bf16[1,256,1280]{2,1,0:T(8,128)(2,1)} copy(bf16[1,256,1280]{2,1,0:T(8,128)(2,1)} %shard_map.91) | data formatting | bytes 1310720
